TPU v7x, 32 devices: a whole 2x2x4 slice. The times are simulated.
32 devices in a mesh: groups: 2 (over y), expert: 4 (over z), tensor: 2 (over x), inner: 2 (over core).
Axes of the slice: x: 2, y: 2, z: 4, core: 2. Of those that a mesh axis runs over, the one named last changes fastest.
Arguments:
- tokens: bfloat16 [1024, 7168], P(('groups', 'expert'), ('tensor', 'inner')), parts along dimension 0, may hold values from -6 to 6
- expert_ids: int32 [1024, 8], P(('groups', 'expert')), parts along dimension 0, may hold values from 0 to 31, all different within a row; in each aligned block of 128 rows (0 to 127, 128 to 255, ...) at most 96 rows name the same one
- gate_weights: float32 [1024, 8], P(('groups', 'expert')), parts along dimension 0, may hold values from 0.05 to 0.45
- base_weights: bfloat16 [3, 1024, 7168], P(None, 'expert', ('tensor', 'inner')), may hold values from -0.0625 to 0.0625
- in_factor: bfloat16 [3840, 7168], P('expert', ('tensor', 'inner')), may hold values from -0.0625 to 0.0625
- out_factors: bfloat16 [2, 3840, 1024], P(None, 'expert', ('tensor', 'inner')), may hold values from -0.375 to 0.375
- ranks: int32 [32], P('expert'), may hold values from 64 to 512, as said below
Outputs:
- mixed: bfloat16 [1024, 7168], P(('groups', 'expert'), ('tensor', 'inner')), parts along dimension 0
There are 2 independent parts, one for each index of `groups`. A program takes and returns all parts, laid end to end along the dimension named above; an argument that names none is the same for every part. Nothing has to cross between parts.
Inputs may be any that keep to these rules, and one draw needn't show every extreme that they name: `expert_ids`: in each aligned block of 128 tokens no expert is chosen more than 96 times, and some expert is chosen exactly 96 times; the experts of one token differ. The ranks of each aligned block of 8 experts sum to exactly 960.
All inputs are finite; a program needn't handle non-finite values.
Results may differ from a plain program's by a relative error of at most 0.023.
Values may be sent and summed in bfloat16 or wider, within the bound.
A program may use at most 64 MiB of HBM per device.

v0:
```python
import jax
import jax.numpy as jnp
from jax import lax
from jax.sharding import PartitionSpec as P

RANK_MAX = 512


def on_device(tokens, expert_ids, gate_weights, base_weights, in_factor, out_factors, ranks):
    tok_rows, feat_slice = tokens.shape
    top_count = expert_ids.shape[1]
    owners = lax.axis_size("expert")
    local_count = ranks.shape[0]
    experts = local_count * owners
    capacity = min(tok_rows, 3 * tok_rows * top_count // experts)
    hidden_slice = out_factors.shape[2]
    width = RANK_MAX
    gathered = lax.all_gather(base_weights, "expert", axis=1, tiled=True)
    partial_value = jnp.einsum(
        "td,gfd->tgf", tokens, gathered[:2], preferred_element_type=jnp.float32
    )
    base_rows = lax.psum_scatter(
        partial_value.astype(jnp.bfloat16), ("tensor", "inner"), scatter_dimension=2, tiled=True
    )
    pairs = tok_rows * top_count
    flat_ids = expert_ids.reshape(pairs)
    columns = lax.broadcasted_iota(jnp.int32, (pairs, experts), 1)
    onehot = (flat_ids[:, None] == columns).astype(jnp.bfloat16)
    row_pos = lax.broadcasted_iota(jnp.int32, (pairs, pairs), 0)
    col_pos = lax.broadcasted_iota(jnp.int32, (pairs, pairs), 1)
    earlier = (row_pos > col_pos).astype(jnp.bfloat16)
    counts = jnp.dot(earlier, onehot, preferred_element_type=jnp.float32)
    slot = jnp.sum(counts * onehot.astype(jnp.float32), axis=1).astype(jnp.int32)
    owner_of = flat_ids // local_count
    member_of = flat_ids % local_count
    target = (member_of * owners + owner_of) * capacity + slot
    source_row = lax.broadcasted_iota(jnp.int32, (pairs,), 0) // top_count
    outgoing = jnp.zeros((local_count * owners * capacity, feat_slice), jnp.bfloat16)
    outgoing = outgoing.at[target].set(tokens[source_row])
    outgoing = outgoing.reshape(local_count, owners, capacity, feat_slice)
    arrived = lax.all_to_all(outgoing, "expert", split_axis=1, concat_axis=1, tiled=True)
    slots = owners * capacity
    arrived = arrived.reshape(local_count, slots, feat_slice)
    starts = jnp.cumsum(ranks) - ranks
    in_pad = jnp.concatenate([in_factor, jnp.zeros((width, feat_slice), jnp.bfloat16)], 0)
    out_pad = jnp.concatenate([out_factors, jnp.zeros((2, width, hidden_slice), jnp.bfloat16)], 1)
    within = lax.broadcasted_iota(jnp.int32, (1, width), 1)
    terms = []
    for member in range(local_count):
        window = lax.dynamic_slice_in_dim(in_pad, starts[member], width, 0)
        terms.append(
            lax.dot_general(
                arrived[member],
                window,
                (((1,), (1,)), ((), ())),
                preferred_element_type=jnp.float32,
            )
        )
    stacked = jnp.stack(
        [
            jnp.where(within < ranks[member], terms[member], jnp.float32(0.0))
            for member in range(local_count)
        ]
    )
    summed = lax.psum(stacked.astype(jnp.bfloat16), ("tensor", "inner"))
    latents = [summed[member] for member in range(local_count)]
    outputs = []
    for member in range(local_count):
        factor = lax.dynamic_slice_in_dim(out_pad, starts[member], width, 1)
        outputs.append(
            jnp.einsum(
                "rc,gcf->rgf", latents[member], factor, preferred_element_type=jnp.float32
            ).astype(jnp.bfloat16)
        )
    replies = jnp.stack(outputs).reshape(local_count, owners, capacity, 2, hidden_slice)
    returned = lax.all_to_all(replies, "expert", split_axis=1, concat_axis=1, tiled=True)
    returned = returned.reshape(local_count * owners * capacity, 2, hidden_slice)
    delta = returned[target].reshape(tok_rows, top_count, 2, hidden_slice)
    summed_rows = base_rows.astype(jnp.float32)[:, None] + delta.astype(jnp.float32)
    hidden = (jax.nn.silu(summed_rows[:, :, 0]) * summed_rows[:, :, 1]).astype(jnp.bfloat16)
    combined = jnp.sum(gate_weights[:, :, None] * hidden.astype(jnp.float32), axis=1).astype(
        jnp.bfloat16
    )
    full_hidden = lax.all_gather(combined, ("tensor", "inner"), axis=1, tiled=True)
    return jnp.dot(full_hidden, gathered[2], preferred_element_type=jnp.float32).astype(
        jnp.bfloat16
    )


def solution(mesh):
    return jax.shard_map(
        on_device,
        mesh=mesh,
        in_specs=(
            P(("groups", "expert"), ("tensor", "inner")),
            P(("groups", "expert"), None),
            P(("groups", "expert"), None),
            P(None, "expert", ("tensor", "inner")),
            P("expert", ("tensor", "inner")),
            P(None, "expert", ("tensor", "inner")),
            P("expert"),
        ),
        out_specs=P(("groups", "expert"), ("tensor", "inner")),
        check_vma=False,
    )
```

profile of v0, /device:TPU:0, one launch (start us, length us, event | category | flops | bytes accessed | tf_op | source)
XLA Modules:
  0.0 655.0 jit_solution(18073991329550731420)
XLA Ops:
  9.0 31.4 %scatter_custom_fusion = bf16[3072,1792]{1,0:T(8,128)(2,1)} fusion(s32[1024]{0:T(1024)S(1)} %bitcast.155, bf16[]{:T(256)} %constant.47.clone.1, bf16[128,1792]{1,0:T(8,128)(2,1)S(1)} %copy-done, s32[1024]{0:T(1024)S(1)} %broadcast_clamp_fusion.1), kind=kCustom, calls=%fused_computation.13 | custom fusion | bytes 11010050 | tf_op jit(solution)/shard_map/scatter | solution.py:39
  40.4 9.6 %copy.42 = bf16[8,4,96,1792]{3,2,0,1:T(8,128)(2,1)} copy(bf16[8,4,96,1792]{3,2,1,0:T(8,128)(2,1)} %bitcast.135) | data formatting | bytes 22020096 | tf_op jit(solution)/shard_map/reshape | solution.py:40
  50.1 6.5 all-to-all-start
  78.3 218.9 %all-to-all-done = bf16[8,4,96,1792]{3,2,0,1:T(8,128)(2,1)} async-done(((bf16[8,4,96,1792]{3,2,0,1:T(8,128)(2,1)}), bf16[8,4,96,1792]{3,2,0,1:T(8,128)(2,1)}, u32[]{:S(2)}, u32[]{:S(2)}) %all-to-all-start) | async-done | bytes 11010080 | tf_op jit(solution)/shard_map/all_to_all | solution.py:41
  297.2 4.9 fusion.91
  302.4 1.9 fusion.50
  304.3 1.9 fusion.48
  306.3 1.9 fusion.46
  308.1 1.9 fusion.44
  310.0 1.9 fusion.42
  311.9 1.9 fusion.40
  313.8 1.9 fusion.38
  315.7 1.9 fusion.36
  318.2 67.3 %all-reduce.4.cloned.1.call-done = bf16[8,384,512]{2,1,0:T(8,128)(2,1)} async-done(((bf16[8,384,512]{2,1,0:T(8,128)(2,1)}), bf16[8,384,512]{2,1,0:T(8,128)(2,1)}) %all-reduce.4.cloned.1.call-update) | async-done | bytes 3145744 | tf_op jit(solution)/shard_map/psum | solution.py:65
  392.1 1.9 copy.54
  394.0 4.7 all-to-all-start.1
  398.7 179.8 %all-gather.2.cloned.1.call-done = bf16[3,1024,1792]{2,1,0:T(8,128)(2,1)} async-done(((bf16[3,256,1792]{2,1,0:T(8,128)(2,1)}), bf16[3,1024,1792]{2,1,0:T(8,128)(2,1)}) %all-gather.2.cloned.1.call-update) | async-done | bytes 11010064 | tf_op jit(solution)/shard_map/all_gather | solution.py:18
  578.5 6.3 fusion.16
  585.0 19.8 %reduce-scatter.2.cloned.1.call-done = bf16[128,2,256]{2,0,1:T(8,128)(2,1)} async-done(((bf16[128,2,1024]{2,0,1:T(8,128)(2,1)}), bf16[128,2,256]{2,0,1:T(8,128)(2,1)}) %reduce-scatter.2.cloned.1.call-update) | async-done | bytes 131088 | tf_op jit(solution)/shard_map/reduce_scatter | solution.py:22
  605.9 2.2 copy.51
  608.0 20.6 %copy.52 = bf16[3072,2,256]{2,1,0:T(2,128)(2,1)} copy(bf16[3072,2,256]{2,0,1:T(8,128)(2,1)S(1)} %bitcast.136) | data formatting | bytes 6291456 | tf_op jit(solution)/shard_map/reshape | solution.py:77
  628.6 6.1 gather_fusion
  638.1 5.8 all_gather.7
  643.9 3.5 fusion.7
  (60 shorter events, 20.2 us)
Async XLA Ops:
  7.4 1.7 copy-start
  50.1 6.5 copy-start.3
  50.1 247.2 %all-to-all-start = ((bf16[8,4,96,1792]{3,2,0,1:T(8,128)(2,1)}), bf16[8,4,96,1792]{3,2,0,1:T(8,128)(2,1)}, u32[]{:S(2)}, u32[]{:S(2)}) async-start(bf16[8,4,96,1792]{3,2,0,1:T(8,128)(2,1)} %copy.42), calls=%async_computation.1 | async-start | bytes 22020096 | tf_op jit(solution)/shard_map/all_to_all | solution.py:41
  56.5 329.0 %all-reduce.4.cloned.1.call-start = ((), (), s32[]{:S(2)}) async-start(), calls=%async_computation.5 | async-start | bytes 6291456 | tf_op jit(solution)/shard_map/psum | solution.py:65
  297.2 5.2 copy-start.5
  317.6 67.9 %copy-start.1 = (bf16[2,960,256]{2,1,0:T(8,128)(2,1)S(1)}, bf16[2,960,256]{2,1,0:T(8,128)(2,1)}, u32[]{:S(2)}) copy-start(bf16[2,960,256]{2,1,0:T(8,128)(2,1)} %param.12) | copy-start | bytes 2949124
  317.6 260.9 %all-gather.2.cloned.1.call-start = ((), (), s32[]{:S(2)}) async-start(), calls=%async_computation.3 | async-start | bytes 13762560 | tf_op jit(solution)/shard_map/all_gather | solution.py:18
  385.5 3.2 copy-start.2
  394.0 211.9 %all-to-all-start.1 = ((bf16[8,4,96,2,256]{4,2,0,3,1:T(8,128)(2,1)}), bf16[8,4,96,2,256]{4,2,0,3,1:T(8,128)(2,1)}, u32[]{:S(2)}, u32[]{:S(2)}) async-start(bf16[8,4,96,2,256]{4,2,0,3,1:T(8,128)(2,1)} %copy.54), calls=%async_computation.2 | async-start | bytes 6291456 | tf_op jit(solution)/shard_map/all_to_all | solution.py:76
  398.7 186.2 %copy-start.4 = (f32[128,8]{0,1:T(8,128)S(1)}, f32[128,8]{0,1:T(8,128)}, u32[]{:S(2)}) copy-start(f32[128,8]{0,1:T(8,128)} %param.9) | copy-start | bytes 12292
  398.7 206.1 %reduce-scatter.2.cloned.1.call-start = ((), (), s32[]{:S(2)}) async-start(), calls=%async_computation.4 | async-start | bytes 655360 | tf_op jit(solution)/shard_map/reduce_scatter | solution.py:22
Sparse Core Ops, SparseCore 0:
  317.7 67.7 all-reduce.3
  585.0 19.7 reduce-scatter.1
Sparse Core Ops, SparseCore 1:
  319.7 258.8 all-gather.1
where the time goes:
time: 664 us; the launch traced here: 655 us
  waiting for transfers between devices  486 us (73%)
  local copies, waits for them, and re-layouts  82.3 us (12%)
  matrix products  31.7 us (5%)
  between operations  30.5 us (5%)
  starting transfers between devices  11.4 us (2%)
  other arithmetic  7.15 us (1%)
    all_to_all x1, waiting for transfers between devices, on_device(): lax.all_to_all(outgoing, 'expert', split_axis=1, concat_axis=1, tiled=True)  219 us
    all_gather x1, waiting for transfers between devices, on_device(): gathered = lax.all_gather(base_weights, 'expert', axis=1, tiled=True)  180 us
    psum x1, waiting for transfers between devices, on_device(): summed = lax.psum(stacked.astype(jnp.bfloat16), ('tensor', 'inner'))  67.3 us
    scatter x1, local copies, waits for them, and re-layouts, on_device(): outgoing = outgoing.at[target].set(tokens[source_row])  31.4 us
    reshape x1, local copies, waits for them, and re-layouts, on_device(): returned.reshape(local_count * owners * capacity, 2, hidden_slice)  20.6 us
    reduce_scatter x1, waiting for transfers between devices, on_device(): lax.psum_scatter(partial_value.astype(jnp.bfloat16), ('tensor', 'inner'),...  19.8 us
    dot_general x8, matrix products, on_device(): lax.dot_general(arrived[member], window, (((1,), (1,)), ((), ())), prefer...  15.2 us
  transfers between devices with their start and end apart: 5, of which 4 were waited for; matrix products, arithmetic and copies ran while one was open for 3% of the time, Pallas kernels for 0%

commit v1 on v0

v1 whole, which is shorter than its diff:
```python
import jax
import jax.numpy as jnp
from jax import lax
from jax.sharding import PartitionSpec as P

FEATURE_AXES = ("tensor", "inner")


def on_device(tokens, expert_ids, gate_weights, base_weights, in_factor, out_factors, ranks):
    tok_rows, feat_slice = tokens.shape
    owners = lax.axis_size("expert")
    local_count = ranks.shape[0]
    experts = local_count * owners
    packed = in_factor.shape[0]
    hidden_rows = base_weights.shape[1]
    hidden_slice = out_factors.shape[2]
    rows = tok_rows * owners

    all_tokens = lax.all_gather(tokens, "expert", axis=0, tiled=True)
    down = lax.all_gather(base_weights[2], "expert", axis=0, tiled=True)

    columns = lax.broadcasted_iota(jnp.int32, (1, 1, experts), 2)
    chosen = expert_ids[:, :, None] == columns
    dense_gates = jnp.sum(jnp.where(chosen, gate_weights[:, :, None], 0.0), axis=1)
    all_gates = lax.all_gather(dense_gates, "expert", axis=0, tiled=True)
    own_gates = lax.dynamic_slice_in_dim(
        all_gates, lax.axis_index("expert") * local_count, local_count, 1
    )

    latent_part = lax.dot_general(
        all_tokens, in_factor, (((1,), (1,)), ((), ())), preferred_element_type=jnp.float32
    ).astype(jnp.bfloat16)
    latent = lax.psum(latent_part, FEATURE_AXES)

    base_part = lax.dot_general(
        all_tokens,
        base_weights[:2].reshape(2 * hidden_rows, feat_slice),
        (((1,), (1,)), ((), ())),
        preferred_element_type=jnp.float32,
    ).astype(jnp.bfloat16)
    base = lax.psum_scatter(base_part, FEATURE_AXES, scatter_dimension=0, tiled=True)
    base = base.reshape(-1, 2, hidden_rows)
    base = lax.all_gather(base, "expert", axis=2, tiled=True)
    base = lax.all_to_all(base, FEATURE_AXES, split_axis=2, concat_axis=0, tiled=True)
    gate_rows = base[:, 0].astype(jnp.float32)
    up_rows = base[:, 1].astype(jnp.float32)

    order = lax.broadcasted_iota(jnp.int32, (local_count, local_count), 0)
    other = lax.broadcasted_iota(jnp.int32, (local_count, local_count), 1)
    ends = jnp.sum(jnp.where(other <= order, ranks[None, :], 0), axis=1)
    where = lax.broadcasted_iota(jnp.int32, (1, packed), 1)
    combined = jnp.zeros((rows, hidden_slice), jnp.float32)
    for member in range(local_count):
        inside = (where >= ends[member] - ranks[member]) & (where < ends[member])
        own = jnp.where(inside, latent, jnp.zeros((), jnp.bfloat16))
        gate = jnp.dot(own, out_factors[0], preferred_element_type=jnp.float32)
        up = jnp.dot(own, out_factors[1], preferred_element_type=jnp.float32)
        hidden = jax.nn.silu(gate_rows + gate) * (up_rows + up)
        combined = combined + own_gates[:, member : member + 1] * hidden
    combined = lax.psum_scatter(
        combined.astype(jnp.bfloat16), "expert", scatter_dimension=0, tiled=True
    )
    full_hidden = lax.all_gather(combined, FEATURE_AXES, axis=1, tiled=True)
    return jnp.dot(full_hidden, down, preferred_element_type=jnp.float32).astype(jnp.bfloat16)


def solution(mesh):
    return jax.shard_map(
        on_device,
        mesh=mesh,
        in_specs=(
            P(("groups", "expert"), ("tensor", "inner")),
            P(("groups", "expert"), None),
            P(("groups", "expert"), None),
            P(None, "expert", ("tensor", "inner")),
            P("expert", ("tensor", "inner")),
            P(None, "expert", ("tensor", "inner")),
            P("expert"),
        ),
        out_specs=P(("groups", "expert"), ("tensor", "inner")),
        check_vma=False,
    )
```

time: 664 us -> 239 us (0.36); the launches traced: 655 us -> 238 us
  waiting for transfers between devices: 486 us -> 129 us
  local copies, waits for them, and re-layouts: 82.3 us -> 12 us
  blocking collectives: 5.79 us -> 38.4 us
  starting transfers between devices: 11.4 us -> 4.31 us
  between operations: 30.5 us -> 23.5 us
    all_to_all x2 -> x1, waiting for transfers between devices: 219 us -> 0.01 us  [on_device(): lax.all_to_all(base, FEATURE_AXES, split_axis=2, concat_axis=0, tiled=True)]
    all_gather x1 -> x2, waiting for transfers between devices: 180 us -> 103 us  [the longest x1 64.5 us: on_device(): down = lax.all_gather(base_weights[2], 'expert', axis=0, tiled=True)]
    psum x1, waiting for transfers between devices: 67.3 us -> 0.01 us  [on_device(): latent = lax.psum(latent_part, FEATURE_AXES)]
    all_gather x1 -> x3, blocking collectives: 5.79 us -> 38.4 us  [the longest x1 17.6 us: on_device(): base = lax.all_gather(base, 'expert', axis=2, tiled=True)]
    scatter x1 -> x0, local copies, waits for them, and re-layouts: 31.4 us -> none  [on_device(): outgoing = outgoing.at[target].set(tokens[source_row])]
    reshape x3 -> x2, local copies, waits for them, and re-layouts: 30.3 us -> 3.32 us  [on_device(): base = base.reshape(-1, 2, hidden_rows)]
    all_to_all x2 -> x1, starting transfers between devices: 11.1 us -> 4.15 us  [on_device(): lax.all_to_all(base, FEATURE_AXES, split_axis=2, concat_axis=0, tiled=True)]
    reduce_scatter x1 -> x2, waiting for transfers between devices: 19.8 us -> 26 us  [the longest x1 17.8 us: on_device(): lax.psum_scatter(combined.astype(jnp.bfloat16), 'expert', scatter_dimensi...]
  transfers between devices with their start and end apart: 5 -> 6, of which waited for: 4 -> 4; matrix products, arithmetic and copies ran while one was open for 3% -> 9% of each run, Pallas kernels for 0% -> 0%
where the time goes in v1:
time: 239 us; the launch traced here: 238 us
  waiting for transfers between devices  129 us (54%)
  blocking collectives  38.4 us (16%)
  matrix products  25.5 us (11%)
  between operations  23.5 us (10%)
  local copies, waits for them, and re-layouts  12 us (5%)
  other arithmetic  5.23 us (2%)
  starting transfers between devices  4.31 us (2%)
    all_gather x1, waiting for transfers between devices, on_device(): down = lax.all_gather(base_weights[2], 'expert', axis=0, tiled=True)  64.5 us
    all_gather x1, waiting for transfers between devices, on_device(): all_tokens = lax.all_gather(tokens, 'expert', axis=0, tiled=True)  38 us
    reduce_scatter x1, waiting for transfers between devices, on_device(): lax.psum_scatter(combined.astype(jnp.bfloat16), 'expert', scatter_dimensi...  17.8 us
    all_gather x1, blocking collectives, on_device(): base = lax.all_gather(base, 'expert', axis=2, tiled=True)  17.6 us
    all_gather x1, blocking collectives, on_device(): all_gates = lax.all_gather(dense_gates, 'expert', axis=0, tiled=True)  13.3 us
    reduce_scatter x1, waiting for transfers between devices, on_device(): lax.psum_scatter(base_part, FEATURE_AXES, scatter_dimension=0, tiled=True)  8.24 us
    all_gather x1, blocking collectives, on_device(): full_hidden = lax.all_gather(combined, FEATURE_AXES, axis=1, tiled=True)  7.47 us
    dot_general x8, matrix products, on_device(): gate = jnp.dot(own, out_factors[0], preferred_element_type=jnp.float32)  7.01 us
  transfers between devices with their start and end apart: 6, of which 4 were waited for; matrix products, arithmetic and copies ran while one was open for 9% of the time, Pallas kernels for 0%

profile of v1, /device:TPU:0, one launch (start us, length us, event | category | flops | bytes accessed | tf_op | source)
XLA Modules:
  0.0 238.4 jit_solution(3506329017285465726)
XLA Ops:
  6.5 0.7 all-gather.4.cloned.1.call-update
  7.3 3.1 %slice.113 = bf16[2,256,1792]{2,1,0:T(8,128)(2,1)} slice(bf16[3,256,1792]{2,1,0:T(8,128)(2,1)} %param.10), slice={[0:2], [0:256], [0:1792]} | slice | bytes 3670016 | tf_op jit(solution)/shard_map/slice | solution.py:37
  15.0 38.0 %all-gather.4.cloned.1.call-done = bf16[512,1792]{1,0:T(8,128)(2,1)} async-done(((bf16[128,1792]{1,0:T(8,128)(2,1)}), bf16[512,1792]{1,0:T(8,128)(2,1)}) %all-gather.4.cloned.1.call-update) | async-done | bytes 1835024 | tf_op jit(solution)/shard_map/all_gather | solution.py:19
  53.1 4.0 %convolution_convert_fusion.1 = bf16[512,512]{1,0:T(8,128)(2,1)} fusion(bf16[512,1792]{1,0:T(8,128)(2,1)} %all-gather.4.cloned.1.call-done, bf16[512,1792]{1,0:T(8,128)(2,1)} %bitcast.111), kind=kOutput, calls=%fused_computation.20 | convolution fusion | flops 939786240 | bytes 4194304 | tf_op jit(solution)/shard_map/dot_general | solution.py:35
  65.0 4.4 %convolution_convert_fusion = bf16[512,960]{0,1:T(8,128)(2,1)} fusion(bf16[512,1792]{1,0:T(8,128)(2,1)} %all-gather.4.cloned.1.call-done, bf16[960,1792]{1,0:T(8,128)(2,1)S(1)} %copy-done), kind=kOutput, calls=%fused_computation.3 | convolution fusion | flops 1762099200 | bytes 6258688 | tf_op jit(solution)/shard_map/dot_general | solution.py:30
  69.5 8.2 %reduce-scatter.3.cloned.1.call-done = bf16[128,512]{1,0:T(8,128)(2,1)} async-done(((bf16[512,512]{1,0:T(8,128)(2,1)}), bf16[128,512]{1,0:T(8,128)(2,1)}) %reduce-scatter.3.cloned.1.call-update) | async-done | bytes 131088 | tf_op jit(solution)/shard_map/reduce_scatter | solution.py:41
  77.7 1.6 reshape.102
  79.3 1.7 copy.22
  81.1 17.6 %all_gather.17 = bf16[128,2,1024]{0,1,2:T(2,128)(2,1)} all-gather(bf16[128,2,256]{0,1,2:T(2,128)(2,1)} %copy.22), channel_id=1, replica_groups=mesh['groups'=2,'expert'=4,'tensor'=2,'inner'=2] {'expert'}, dimensions={2}, use_global_device_ids=true | all-gather | bytes 655360 | tf_op jit(solution)/shard_map/all_gather | solution.py:43
  98.7 4.1 %all-to-all-start = ((bf16[128,2,1024]{0,1,2:T(2,128)(2,1)}), bf16[128,2,1024]{0,1,2:T(2,128)(2,1)}, u32[]{:S(2)}, u32[]{:S(2)}) async-start(bf16[128,2,1024]{0,1,2:T(2,128)(2,1)} %all_gather.17), calls=%async_computation.1 | async-start | bytes 1048576 | tf_op jit(solution)/shard_map/all_to_all | solution.py:44
  106.1 13.3 %all_gather.15 = f32[512,32]{0,1:T(8,128)S(1)} all-gather(f32[128,32]{0,1:T(8,128)S(1)} %select_reduce_fusion), channel_id=1, replica_groups=mesh['groups'=2,'expert'=4,'tensor'=2,'inner'=2] {'expert'}, dimensions={0}, use_global_device_ids=true | all-gather | bytes 81920 | tf_op jit(solution)/shard_map/all_gather | solution.py:25
  120.6 2.0 copy.23
  122.6 2.2 convert_add_fusion.13
  129.7 0.7 fusion.18
  131.2 0.7 fusion.17
  131.9 0.7 fusion.16
  132.6 0.7 fusion.15
  134.0 0.7 fusion.13
  134.7 1.6 fusion.28
  136.4 2.2 slice.141
  138.6 17.8 %reduce-scatter.5.cloned.1.call-done = bf16[128,256]{1,0:T(8,128)(2,1)} async-done(((bf16[512,256]{1,0:T(8,128)(2,1)}), bf16[128,256]{1,0:T(8,128)(2,1)}) %reduce-scatter.5.cloned.1.call-update) | async-done | bytes 65552 | tf_op jit(solution)/shard_map/reduce_scatter | solution.py:60
  156.4 7.5 %all_gather.18 = bf16[128,1024]{1,0:T(8,128)(2,1)} all-gather(bf16[128,256]{1,0:T(8,128)(2,1)} %reduce-scatter.5.cloned.1.call-done), channel_id=1, replica_groups=mesh['groups'=2,'expert'=4,'tensor'=2,'inner'=2] {'tensor','inner'}, dimensions={1}, use_global_device_ids=true | all-gather | bytes 327680 | tf_op jit(solution)/shard_map/all_gather | solution.py:63
  163.8 64.5 %all-gather.6.cloned.1.call-done = bf16[1,1024,1792]{2,1,0:T(8,128)(2,1)} async-done(((bf16[1,256,1792]{2,1,0:T(8,128)(2,1)}), bf16[1,1024,1792]{2,1,0:T(8,128)(2,1)}) %all-gather.6.cloned.1.call-update) | async-done | bytes 3670032 | tf_op jit(solution)/shard_map/all_gather | solution.py:20
  228.3 3.6 %fusion.2 = bf16[128,1792]{1,0:T(8,128)(2,1)} fusion(bf16[128,1024]{1,0:T(8,128)(2,1)} %all_gather.18, bf16[1,1024,1792]{2,1,0:T(8,128)(2,1)} %all-gather.6.cloned.1.call-done), kind=kOutput, calls=%fused_computation.2 | convolution fusion | flops 469991424 | bytes 4390912 | tf_op jit(solution)/shard_map/dot_general | solution.py:64
  (47 shorter events, 13.1 us)
Async XLA Ops:
  6.5 58.5 %copy-start = (bf16[960,1792]{1,0:T(8,128)(2,1)S(1)}, bf16[960,1792]{1,0:T(8,128)(2,1)}, u32[]{:S(2)}) copy-start(bf16[960,1792]{1,0:T(8,128)(2,1)} %param.11) | copy-start | bytes 10321924
  6.5 46.5 %all-gather.4.cloned.1.call-start = ((), (), s32[]{:S(2)}) async-start(), calls=%async_computation.3 | async-start | bytes 2293760 | tf_op jit(solution)/shard_map/all_gather | solution.py:19
  7.3 3.2 %copy-start.2 = (s32[8]{0:T(128)S(1)}, s32[8]{0:T(128)}, u32[]{:S(2)}) copy-start(s32[8]{0:T(128)} %param.13) | copy-start | bytes 100
  7.3 70.5 %reduce-scatter.3.cloned.1.call-start = ((), (), s32[]{:S(2)}) async-start(), calls=%async_computation.4 | async-start | bytes 655360 | tf_op jit(solution)/shard_map/reduce_scatter | solution.py:41
  53.1 11.9 %copy-start.3 = (f32[128,8]{0,1:T(8,128)S(1)}, f32[128,8]{0,1:T(8,128)}, u32[]{:S(2)}) copy-start(f32[128,8]{0,1:T(8,128)} %param.9) | copy-start | bytes 12292
  53.1 11.9 %copy-start.4 = (s32[128,8]{0,1:T(8,128)S(1)}, s32[128,8]{0,1:T(8,128)}, u32[]{:S(2)}) copy-start(s32[128,8]{0,1:T(8,128)} %param.8) | copy-start | bytes 12292
  57.1 65.5 %all-reduce.2.cloned.1.call-start = ((), (), s32[]{:S(2)}) async-start(), calls=%async_computation.5 | async-start | bytes 1966080 | tf_op jit(solution)/shard_map/psum | solution.py:33
  98.7 21.9 %all-to-all-start = ((bf16[128,2,1024]{0,1,2:T(2,128)(2,1)}), bf16[128,2,1024]{0,1,2:T(2,128)(2,1)}, u32[]{:S(2)}, u32[]{:S(2)}) async-start(bf16[128,2,1024]{0,1,2:T(2,128)(2,1)} %all_gather.17), calls=%async_computation.1 | async-start | bytes 1048576 | tf_op jit(solution)/shard_map/all_to_all | solution.py:44
  102.9 53.5 %reduce-scatter.5.cloned.1.call-start = ((), (), s32[]{:S(2)}) async-start(), calls=%async_computation.6 | async-start | bytes 327680 | tf_op jit(solution)/shard_map/reduce_scatter | solution.py:60
  122.6 2.2 copy-start.1
  122.6 2.2 copy-start.5
  122.6 2.2 copy-start.6
  136.3 92.0 %all-gather.6.cloned.1.call-start = ((), (), s32[]{:S(2)}) async-start(), calls=%async_computation.7 | async-start | bytes 4587520 | tf_op jit(solution)/shard_map/all_gather | solution.py:20
Sparse Core Ops, SparseCore 0:
  8.9 44.0 all-gather.3
  57.2 20.4 reduce-scatter.2
  80.3 39.6 all-reduce.1
  136.4 19.8 reduce-scatter.4
  157.9 70.4 all-gather.5

commit v2 on v1

--- a/solution.py
+++ b/solution.py
@@ -1,9 +1,357 @@
+import functools
 import jax
 import jax.numpy as jnp
 from jax import lax
+from jax.experimental import pallas as pl
+from jax.experimental.pallas import tpu as pltpu
 from jax.sharding import PartitionSpec as P
 
 FEATURE_AXES = ("tensor", "inner")
+MESH = pl.DeviceIdType.MESH
+BF16 = jnp.bfloat16
+F32 = jnp.float32
+
+
+def nearest(at, k, n):
+    both = jnp.minimum(at, n - 1 - at)
+    near = (k + 1) // 2
+    left_near = k % 2
+    far = k - both
+    left_far = (at > n - 1 - at).astype(jnp.int32)
+    inside = (k <= 2 * both).astype(jnp.int32)
+    dist = inside * near + (1 - inside) * far
+    left = inside * left_near + (1 - inside) * left_far
+    return at + dist * (1 - 2 * left)
+
+
+def fused(
+    n, plane, tokens, gates, mask, base_weights, in_factor, out_factors, out,
+    all_tok, base_w, in_w, out_w, own_gates, part, a_got, half, bl_got, bb_got, lat, piece,
+    base_all, delta, comb, comb_got, full,
+    load_sem, tok_l, tok_r, tok_got, gate_s, gate_r, a_s, a_r, bl_s, bl_r, bb_s, bb_r, c_s, c_r,
+    base_s, base_r, comb_s, comb_r, ag_s, ag_r,
+):
+    me = lax.axis_index("expert")
+    x = lax.axis_index("tensor")
+    c = lax.axis_index("inner")
+    ti = x * 2 + c
+    rows = tokens.shape[0]
+    packed = in_factor.shape[0]
+    wide = bl_got.shape[2]
+    unit = base_weights.shape[1]
+    local = mask.shape[0]
+    hid = out_factors.shape[2]
+    two, four = rows // 2, rows // 4
+
+    def rdma(src, dst, send, recv, **where):
+        return pltpu.make_async_remote_copy(
+            src_ref=src, dst_ref=dst, send_sem=send, recv_sem=recv,
+            device_id=where, device_id_type=MESH,
+        )
+
+    barrier = pltpu.get_barrier_semaphore()
+    for de in range(n):
+        for dt in range(plane):
+            if de or dt:
+                to = lax.rem(ti + dt, plane)
+                pl.semaphore_signal(
+                    barrier, inc=1,
+                    device_id={"expert": lax.rem(me + de, n), "tensor": to // 2, "inner": lax.rem(to, 2)},
+                    device_id_type=MESH,
+                )
+    loads = [
+        pltpu.make_async_copy(tokens, all_tok.at[me], load_sem.at[0]),
+        pltpu.make_async_copy(in_factor, in_w, load_sem.at[1]),
+        pltpu.make_async_copy(base_weights.at[pl.ds(0, 2)], base_w, load_sem.at[2]),
+        pltpu.make_async_copy(out_factors, out_w, load_sem.at[3]),
+        pltpu.make_async_copy(
+            gates.at[pl.ds(pl.multiple_of(me * local, local), local)], own_gates.at[me], load_sem.at[4]
+        ),
+    ]
+    for load in loads:
+        load.start()
+    pl.semaphore_wait(barrier, n * plane - 1)
+
+    def to_right(b, src):
+        return rdma(src, all_tok.at[b], tok_r.at[b], tok_got.at[b], expert=lax.rem(me + 1, n))
+
+    def to_left(b, src):
+        return rdma(src, all_tok.at[b], tok_l.at[b], tok_got.at[b], expert=lax.rem(me + n - 1, n))
+
+    @pl.when(me + 1 < n)
+    def _():
+        to_right(me, tokens).start()
+
+    @pl.when(me >= 1)
+    def _():
+        to_left(me, tokens).start()
+
+    def gate_copy(step):
+        p = lax.rem(me + step, n)
+        return rdma(
+            gates.at[pl.ds(pl.multiple_of(p * local, local), local)], own_gates.at[me],
+            gate_s.at[p], gate_r.at[me], expert=p,
+        )
+
+    for step in range(1, n):
+        gate_copy(step).start()
+
+    mine = pl.multiple_of(c * two, two)
+    other = pl.multiple_of((1 - c) * two, two)
+
+    def a_copy(b):
+        return rdma(part.at[b, pl.ds(other, two)], a_got.at[b], a_s.at[b], a_r.at[b], inner=1 - c)
+
+    def bl_copy(b):
+        return rdma(
+            half.at[b, :, pl.ds(0, wide)], bl_got.at[b], bl_s.at[b], bl_r.at[b], tensor=1 - x
+        )
+
+    def bb_copy(b):
+        return rdma(
+            half.at[b, pl.ds(pl.multiple_of((1 - x) * four, four), four), pl.ds(wide, 2 * unit)],
+            bb_got.at[b], bb_s.at[b], bb_r.at[b], tensor=1 - x,
+        )
+
+    def c_copy(b):
+        return rdma(lat.at[b, pl.ds(mine, two)], lat.at[b, pl.ds(mine, two)], c_s.at[b], c_r.at[b], inner=1 - c)
+
+    quarter = c * 2 + x
+
+    def base_copy(b, e):
+        return rdma(
+            piece.at[b], base_all.at[b, pl.ds(pl.multiple_of(quarter * four, four), four)],
+            base_s.at[b, e], base_r.at[b, quarter], expert=e, tensor=me // 2, inner=lax.rem(me, 2),
+        )
+
+    for load in loads:
+        load.wait()
+
+    def phase(k, carry):
+        b = nearest(me, jnp.minimum(k, n - 1), n)
+
+        @pl.when(k < n)
+        def _():
+            @pl.when(k >= 1)
+            def _():
+                to_right(b, all_tok.at[b]).wait_recv()
+
+                @pl.when((b < me) & (me + 1 < n))
+                def _():
+                    to_right(b, all_tok.at[b]).start()
+
+                @pl.when((b > me) & (me >= 1))
+                def _():
+                    to_left(b, all_tok.at[b]).start()
+
+            t = all_tok[b]
+            nt = (((1,), (1,)), ((), ()))
+            value = lax.dot_general(t, in_w[...], nt, preferred_element_type=F32).astype(BF16)
+            if wide > packed:
+                part[b, :, packed:wide] = jnp.zeros((rows, wide - packed), BF16)
+            part[b, :, 0:packed] = value
+            for g in range(2):
+                value = lax.dot_general(t, base_w[g], nt, preferred_element_type=F32)
+                part[b, :, wide + g * unit : wide + (g + 1) * unit] = value.astype(BF16)
+            a_copy(b).start()
+
+        @pl.when((k >= 1) & (k <= n))
+        def _():
+            p = nearest(me, jnp.maximum(k - 1, 0), n)
+            bb_copy(p).wait_recv()
+            own = half[p, pl.ds(pl.multiple_of(x * four, four), four), wide : wide + 2 * unit]
+            piece[p] = (own.astype(F32) + bb_got[p].astype(F32)).astype(BF16)
+            for e in range(n):
+                here = (me == e) & (ti == me)
+
+                @pl.when(jnp.logical_not(here))
+                def _():
+                    base_copy(p, e).start()
+
+                @pl.when(here)
+                def _():
+                    base_all[p, pl.ds(pl.multiple_of(quarter * four, four), four)] = piece[p]
+
+            bl_copy(p).wait_recv()
+            lat[p, pl.ds(mine, two)] = (
+                half[p, :, 0:wide].astype(F32) + bl_got[p].astype(F32)
+            ).astype(BF16)
+            c_copy(p).start()
+
+        @pl.when(k < n)
+        def _():
+            a_copy(b).wait_recv()
+            half[b] = (part[b, pl.ds(mine, two)].astype(F32) + a_got[b].astype(F32)).astype(BF16)
+            bb_copy(b).start()
+            bl_copy(b).start()
+
+        @pl.when(k >= 2)
+        def _():
+            p = nearest(me, jnp.maximum(k - 2, 0), n)
+            rdma(
+                lat.at[p, pl.ds(other, two)], lat.at[p, pl.ds(other, two)], c_s.at[p], c_r.at[p],
+                inner=1 - c,
+            ).wait_recv()
+            value = lat[p, :, 0:packed]
+            for j in range(local):
+                own = value * mask[j : j + 1, :].astype(BF16)
+                for g in range(2):
+                    delta[p, j, :, g * hid : (g + 1) * hid] = jnp.dot(
+                        own, out_w[g], preferred_element_type=F32
+                    ).astype(BF16)
+
+        return carry
+
+    lax.fori_loop(0, n + 2, phase, 0)
+
+    for step in range(1, n):
+        p = lax.rem(me + step, n)
+        rdma(own_gates.at[p], own_gates.at[p], gate_s.at[p], gate_r.at[p], expert=p).wait_recv()
+
+    def comb_copy(b):
+        return rdma(comb.at[b], comb_got.at[me], comb_s.at[b], comb_r.at[me], expert=b)
+
+    def finish(k, carry):
+        b = nearest(ti, k, n)
+        for q in range(plane):
+            @pl.when(jnp.logical_not((me == ti) & (quarter == q)))
+            def _():
+                spot = base_all.at[b, pl.ds(q * four, four)]
+                rdma(spot, spot, base_s.at[b, 0], base_r.at[b, q], tensor=1 - x).wait_recv()
+
+        pick = (
+            lax.broadcasted_iota(jnp.int32, (local, 128), 0)
+            == lax.broadcasted_iota(jnp.int32, (local, 128), 1)
+        ).astype(F32)
+        weight = lax.dot_general(
+            own_gates[b], pick, (((0,), (0,)), ((), ())),
+            preferred_element_type=F32, precision=lax.Precision.HIGHEST,
+        )
+        gate_base = base_all[b, :, 0:unit].astype(F32)
+        up_base = base_all[b, :, unit : 2 * unit].astype(F32)
+        total = jnp.zeros((rows, hid), F32)
+        for j in range(local):
+            v = gate_base + delta[b, j, :, 0:hid].astype(F32)
+            u = up_base + delta[b, j, :, hid : 2 * hid].astype(F32)
+            total = total + weight[:, j : j + 1] * (v / (1.0 + jnp.exp(-v)) * u)
+        comb[b] = total.astype(BF16)
+
+        @pl.when(b != me)
+        def _():
+            comb_copy(b).start()
+
+        return carry
+
+    lax.fori_loop(0, n, finish, 0)
+
+    total = comb[me].astype(F32)
+    for step in range(1, n):
+        p = lax.rem(me + step, n)
+        rdma(comb_got.at[p], comb_got.at[p], comb_s.at[p], comb_r.at[p], expert=p).wait_recv()
+        total = total + comb_got[p].astype(F32)
+    full[ti] = total.astype(BF16)
+
+    def ag_copy(step):
+        to = lax.rem(ti + step, plane)
+        return rdma(
+            full.at[ti], full.at[ti], ag_s.at[to], ag_r.at[ti], tensor=to // 2, inner=lax.rem(to, 2)
+        )
+
+    for step in range(1, plane):
+        ag_copy(step).start()
+    for step in range(1, plane):
+        p = lax.rem(ti + step, plane)
+        rdma(full.at[p], full.at[p], ag_s.at[p], ag_r.at[p], tensor=1 - x).wait_recv()
+    for q in range(plane):
+        out[:, q * hid : (q + 1) * hid] = full[q]
+
+    for b in range(n):
+        @pl.when((b <= me) & (me + 1 < n))
+        def _():
+            to_right(b, all_tok.at[b]).wait_send()
+
+        @pl.when((b >= me) & (me >= 1))
+        def _():
+            to_left(b, all_tok.at[b]).wait_send()
+
+        a_copy(b).wait_send()
+        bl_copy(b).wait_send()
+        bb_copy(b).wait_send()
+        c_copy(b).wait_send()
+        for e in range(n):
+            @pl.when(jnp.logical_not((me == e) & (ti == me)))
+            def _():
+                base_copy(b, e).wait_send()
+
+        @pl.when(b != me)
+        def _():
+            comb_copy(b).wait_send()
+
+    for step in range(1, n):
+        gate_copy(step).wait_send()
+    for step in range(1, plane):
+        ag_copy(step).wait_send()
+
+
+def hidden_of(tokens, dense_gates, base_weights, in_factor, out_factors, ranks):
+    rows, feat = tokens.shape
+    n = lax.axis_size("expert")
+    plane = lax.axis_size("tensor") * lax.axis_size("inner")
+    local = ranks.shape[0]
+    packed = in_factor.shape[0]
+    wide = -(-packed // 128) * 128
+    unit = base_weights.shape[1]
+    hid = out_factors.shape[2]
+    order = lax.broadcasted_iota(jnp.int32, (local, local), 0)
+    other = lax.broadcasted_iota(jnp.int32, (local, local), 1)
+    ends = jnp.sum(jnp.where(other <= order, ranks[None, :], 0), axis=1)[:, None]
+    place = lax.broadcasted_iota(jnp.int32, (local, packed), 1)
+    mask = ((place < ends) & (place >= ends - ranks[:, None])).astype(F32)
+    two, four = rows // 2, rows // 4
+    vmem = pltpu.VMEM
+    dma = pltpu.SemaphoreType.DMA
+    return pl.pallas_call(
+        functools.partial(fused, n, plane),
+        out_shape=jax.ShapeDtypeStruct((rows, plane * hid), BF16),
+        in_specs=[
+            pl.BlockSpec(memory_space=pl.ANY),
+            pl.BlockSpec(memory_space=vmem),
+            pl.BlockSpec(memory_space=vmem),
+            pl.BlockSpec(memory_space=pl.ANY),
+            pl.BlockSpec(memory_space=pl.ANY),
+            pl.BlockSpec(memory_space=pl.ANY),
+        ],
+        out_specs=pl.BlockSpec(memory_space=vmem),
+        scratch_shapes=[
+            vmem((n, rows, feat), BF16),
+            vmem((2, unit, feat), BF16),
+            vmem((packed, feat), BF16),
+            vmem((2, packed, hid), BF16),
+            vmem((n, local, rows), F32),
+            vmem((n, rows, wide + 2 * unit), BF16),
+            vmem((n, two, wide + 2 * unit), BF16),
+            vmem((n, two, wide + 2 * unit), BF16),
+            vmem((n, two, wide), BF16),
+            vmem((n, four, 2 * unit), BF16),
+            vmem((n, rows, wide), BF16),
+            vmem((n, four, 2 * unit), BF16),
+            vmem((n, rows, 2 * unit), BF16),
+            vmem((n, local, rows, 2 * hid), BF16),
+            vmem((n, rows, hid), BF16),
+            vmem((n, rows, hid), BF16),
+            vmem((plane, rows, hid), BF16),
+            dma((5,)),
+            dma((n,)), dma((n,)), dma((n,)), dma((n,)), dma((n,)),
+            dma((n,)), dma((n,)), dma((n,)), dma((n,)), dma((n,)), dma((n,)), dma((n,)), dma((n,)),
+            dma((n, n)), dma((n, plane)), dma((n,)), dma((n,)), dma((plane,)), dma((plane,)),
+        ],
+        compiler_params=pltpu.CompilerParams(
+            collective_id=0, has_side_effects=True, vmem_limit_bytes=48 * 1024 * 1024
+        ),
+        cost_estimate=pl.CostEstimate(
+            flops=60_000_000_000, bytes_accessed=20_000_000, transcendentals=0
+        ),
+    )(tokens, dense_gates.T, mask, base_weights, in_factor, out_factors)
 
 
 def on_device(tokens, expert_ids, gate_weights, base_weights, in_factor, out_factors, ranks):
@@ -16,12 +364,18 @@
     hidden_slice = out_factors.shape[2]
     rows = tok_rows * owners
 
-    all_tokens = lax.all_gather(tokens, "expert", axis=0, tiled=True)
     down = lax.all_gather(base_weights[2], "expert", axis=0, tiled=True)
 
     columns = lax.broadcasted_iota(jnp.int32, (1, 1, experts), 2)
     chosen = expert_ids[:, :, None] == columns
     dense_gates = jnp.sum(jnp.where(chosen, gate_weights[:, :, None], 0.0), axis=1)
+    tensor, inner = lax.axis_size("tensor"), lax.axis_size("inner")
+    if tensor == 2 and inner == 2 and owners == tensor * inner and tok_rows % 64 == 0:
+        full_hidden = hidden_of(
+            tokens, dense_gates, base_weights, in_factor, out_factors, ranks
+        )
+        return jnp.dot(full_hidden, down, preferred_element_type=jnp.float32).astype(jnp.bfloat16)
+    all_tokens = lax.all_gather(tokens, "expert", axis=0, tiled=True)
     all_gates = lax.all_gather(dense_gates, "expert", axis=0, tiled=True)
     own_gates = lax.dynamic_slice_in_dim(
         all_gates, lax.axis_index("expert") * local_count, local_count, 1

time: 239 us -> 154 us (0.64)
  waiting for transfers between devices: 129 us -> 0.04 us
  Pallas kernels: 0 us -> 128 us
  blocking collectives: 38.4 us -> 0 us
  matrix products: 25.5 us -> 3.46 us
  between operations: 23.5 us -> 13.4 us
  local copies, waits for them, and re-layouts: 12 us -> 6.15 us
  starting transfers between devices: 4.31 us -> 0.01 us
  other arithmetic: 5.23 us -> 2.23 us
    pallas_call x0 -> x1, Pallas kernels: none -> 128 us  [hidden_of(): pl.pallas_call(functools.partial(fused, n, plane), out_shape=jax.ShapeDty...]
    all_gather x1, waiting for transfers between devices: 64.5 us -> 0.02 us  [on_device(): down = lax.all_gather(base_weights[2], 'expert', axis=0, tiled=True)]
    all_gather x3 -> x0, blocking collectives: 38.4 us -> none  [the longest x1 17.6 us: on_device(): base = lax.all_gather(base, 'expert', axis=2, tiled=True)]
    all_gather x1 -> x0, waiting for transfers between devices: 38 us -> none  [on_device(): all_tokens = lax.all_gather(tokens, 'expert', axis=0, tiled=True)]
    reduce_scatter x2 -> x0, waiting for transfers between devices: 26 us -> none  [the longest x1 17.8 us: on_device(): lax.psum_scatter(combined.astype(jnp.bfloat16), 'expert', scatter_dimensi...]
    dot_general x18 -> x0, matrix products: 21.9 us -> none  [the longest x8 7.01 us: on_device(): gate = jnp.dot(own, out_factors[0], preferred_element_type=jnp.float32)]
    and x8 -> x0, other arithmetic: 5.1 us -> none  [on_device(): inside = (where >= ends[member] - ranks[member]) & (where < ends[member])]
    slice x4 -> x0, local copies, waits for them, and re-layouts: 4.52 us -> none  [the longest x1 3.12 us: on_device(): base_weights[:2].reshape(2 * hidden_rows, feat_slice)]
  transfers between devices with their start and end apart: 6 -> 1, of which waited for: 4 -> 0; matrix products, arithmetic and copies ran while one was open for 9% -> 1% of each run, Pallas kernels for 0% -> 84%
where the time goes in v2:
time: 154 us
  Pallas kernels  128 us (83%)
  between operations  13.4 us (9%)
  local copies, waits for them, and re-layouts  6.15 us (4%)
  matrix products  3.46 us (2%)
  other arithmetic  2.23 us (1%)
    pallas_call x1, Pallas kernels, hidden_of(): pl.pallas_call(functools.partial(fused, n, plane), out_shape=jax.ShapeDty...  128 us
    unnamed x6, local copies, waits for them, and re-layouts  3.99 us
    dot_general x1, matrix products, on_device(): jnp.dot(full_hidden, down, preferred_element_type=jnp.float32)  3.46 us
  transfers between devices with their start and end apart: 1, of which 0 were waited for; matrix products, arithmetic and copies ran while one was open for 1% of the time, Pallas kernels for 84%

profile of v2, /device:TPU:0, one launch (start us, length us, event | category | flops | bytes accessed | tf_op | source)
XLA Modules:
  0.0 153.6 jit_solution(1143312470954320988)
XLA Ops:
  6.5 0.0 all-gather.3.cloned.1.call-start
  6.5 2.2 %slice.3 = bf16[1,256,1792]{2,1,0:T(8,128)(2,1)} slice(bf16[3,256,1792]{2,1,0:T(8,128)(2,1)} %base_weights.1), slice={[2:3], [0:256], [0:1792]} | slice | bytes 1835008 | tf_op jit(solution)/shard_map/slice | solution.py:367
  8.7 0.0 all-gather.3.cloned.1.call-update
  8.7 0.8 select_reduce_fusion.1
  9.5 0.7 sub.4
  10.2 0.1 fusion.6.mask
  10.2 0.7 select_reduce_fusion
  11.0 0.0 copy-start
  11.0 1.8 %copy-done = bf16[3,256,1792]{2,1,0:T(8,128)(2,1)S(1)} copy-done((bf16[3,256,1792]{2,1,0:T(8,128)(2,1)S(1)}, bf16[3,256,1792]{2,1,0:T(8,128)(2,1)}, u32[]{:S(2)}) %copy-start) | copy-done | bytes 2752536
  12.7 0.0 copy-start.1
  12.7 1.2 copy-done.1
  13.9 0.0 copy-start.2
  13.9 1.0 copy-done.2
  15.0 128.3 %shard_map.73 = bf16[128,1024]{1,0:T(8,128)(2,1)S(1)} custom-call(bf16[128,1792]{1,0:T(8,128)(2,1)S(1)} %copy-done.2, f32[32,128]{1,0:T(8,128)S(1)} %bitcast.7, f32[8,960]{1,0:T(8,128)S(1)} %fusion.6.mask, bf16[3,256,1792]{2,1,0:T(8,128)(2,1)S(1)} %copy-done, bf16[960,1792]{1,0:T(8,128)(2,1)} %in_factor.1, bf16[2,960,256]{2,1,0:T(8,128)(2,1)S(1)} %copy-done.1), custom_call_target="tpu_custom_call" | custom-call | flops 60000002048 | bytes 20000000 | tf_op jit(solution)/shard_map/pallas_call | solution.py:313
  143.2 0.0 all-gather.3.cloned.1.call-done
  143.3 3.5 %fusion.2 = bf16[128,1792]{1,0:T(8,128)(2,1)} fusion(bf16[128,1024]{1,0:T(8,128)(2,1)S(1)} %shard_map.73, bf16[1,1024,1792]{2,1,0:T(8,128)(2,1)} %all-gather.3.cloned.1.call-done), kind=kOutput, calls=%fused_computation.2 | convolution fusion | flops 469991424 | bytes 4390912 | tf_op jit(solution)/shard_map/dot_general | solution.py:377
Async XLA Ops:
  6.5 136.7 %all-gather.3.cloned.1.call-start = ((), (), s32[]{:S(2)}) async-start(), calls=%async_computation | async-start | bytes 4587520 | tf_op jit(solution)/shard_map/all_gather | solution.py:367
  11.0 1.8 %copy-start = (bf16[3,256,1792]{2,1,0:T(8,128)(2,1)S(1)}, bf16[3,256,1792]{2,1,0:T(8,128)(2,1)}, u32[]{:S(2)}) copy-start(bf16[3,256,1792]{2,1,0:T(8,128)(2,1)} %base_weights.1) | copy-start | bytes 8257540
  12.7 1.2 copy-start.1
  13.9 1.0 copy-start.2
Sparse Core Ops, SparseCore 0:
  8.9 104.1 all-gather.2

commit v3 on v2

--- a/solution.py
+++ b/solution.py
@@ -27,14 +27,16 @@
 def fused(
     n, plane, tokens, gates, mask, base_weights, in_factor, out_factors, out,
     all_tok, base_w, in_w, out_w, own_gates, part, a_got, half, bl_got, bb_got, lat, piece,
-    base_all, delta, comb, comb_got, full,
+    base_all, delta, comb, comb_got, full, down_w, acc,
     load_sem, tok_l, tok_r, tok_got, gate_s, gate_r, a_s, a_r, bl_s, bl_r, bb_s, bb_r, c_s, c_r,
-    base_s, base_r, comb_s, comb_r, ag_s, ag_r,
+    base_s, base_r, comb_s, comb_r, ag_s, ag_r, wl_s, wr_s, w_got, wy_s, wy_got,
 ):
     me = lax.axis_index("expert")
     x = lax.axis_index("tensor")
     c = lax.axis_index("inner")
+    y = lax.axis_index("groups")
     ti = x * 2 + c
+    cuts = w_got.shape[1]
     rows = tokens.shape[0]
     packed = in_factor.shape[0]
     wide = bl_got.shape[2]
@@ -59,6 +61,7 @@
                     device_id={"expert": lax.rem(me + de, n), "tensor": to // 2, "inner": lax.rem(to, 2)},
                     device_id_type=MESH,
                 )
+    pl.semaphore_signal(barrier, inc=1, device_id={"groups": 1 - y}, device_id_type=MESH)
     loads = [
         pltpu.make_async_copy(tokens, all_tok.at[me], load_sem.at[0]),
         pltpu.make_async_copy(in_factor, in_w, load_sem.at[1]),
@@ -67,10 +70,11 @@
         pltpu.make_async_copy(
             gates.at[pl.ds(pl.multiple_of(me * local, local), local)], own_gates.at[me], load_sem.at[4]
         ),
+        pltpu.make_async_copy(base_weights.at[2], down_w.at[me], load_sem.at[5]),
     ]
     for load in loads:
         load.start()
-    pl.semaphore_wait(barrier, n * plane - 1)
+    pl.semaphore_wait(barrier, n * plane)
 
     def to_right(b, src):
         return rdma(src, all_tok.at[b], tok_r.at[b], tok_got.at[b], expert=lax.rem(me + 1, n))
@@ -126,6 +130,62 @@
 
     for load in loads:
         load.wait()
+
+    bit = unit // 2 // cuts
+
+    def span(w, half_at):
+        return pl.ds(pl.multiple_of(half_at * (unit // 2) + w * bit, bit), bit)
+
+    def w_right(b, w, src):
+        return rdma(src, down_w.at[b, span(w, y)], wr_s.at[b, w], w_got.at[b, w], expert=lax.rem(me + 1, n))
+
+    def w_left(b, w, src):
+        return rdma(src, down_w.at[b, span(w, y)], wl_s.at[b, w], w_got.at[b, w], expert=lax.rem(me + n - 1, n))
+
+    def w_side(b, w):
+        spot = down_w.at[b, span(w, y)]
+        return rdma(spot, spot, wy_s.at[b, w], wy_got.at[b, w], groups=1 - y)
+
+    def w_side_wait(b):
+        for w in range(cuts):
+            spot = down_w.at[b, span(w, 1 - y)]
+            rdma(spot, spot, wy_s.at[b, w], wy_got.at[b, w], groups=1 - y).wait_recv()
+
+    def w_begin():
+        for w in range(cuts):
+            @pl.when(me + 1 < n)
+            def _():
+                w_right(me, w, down_w.at[me, span(w, y)]).start()
+
+            @pl.when(me >= 1)
+            def _():
+                w_left(me, w, down_w.at[me, span(w, y)]).start()
+
+    def w_step(dist):
+        for w in range(cuts):
+            @pl.when(me >= dist)
+            def _():
+                b = lax.rem(me - dist + n, n)
+                spot = down_w.at[b, span(w, y)]
+                w_right(b, w, spot).wait_recv()
+
+                @pl.when(me + 1 < n)
+                def _():
+                    w_right(b, w, spot).start()
+
+                w_side(b, w).start()
+
+            @pl.when(me + dist < n)
+            def _():
+                b = lax.rem(me + dist, n)
+                spot = down_w.at[b, span(w, y)]
+                w_left(b, w, spot).wait_recv()
+
+                @pl.when(me >= 1)
+                def _():
+                    w_left(b, w, spot).start()
+
+                w_side(b, w).start()
 
     def phase(k, carry):
         b = nearest(me, jnp.minimum(k, n - 1), n)
@@ -203,6 +263,7 @@
         return carry
 
     lax.fori_loop(0, n + 2, phase, 0)
+    w_begin()
 
     for step in range(1, n):
         p = lax.rem(me + step, n)
@@ -242,7 +303,9 @@
 
         return carry
 
-    lax.fori_loop(0, n, finish, 0)
+    lax.fori_loop(0, n - 1, finish, 0)
+    w_step(1)
+    finish(n - 1, 0)
 
     total = comb[me].astype(F32)
     for step in range(1, n):
@@ -259,11 +322,19 @@
 
     for step in range(1, plane):
         ag_copy(step).start()
+    for dist in range(2, n - 1):
+        w_step(dist)
     for step in range(1, plane):
         p = lax.rem(ti + step, plane)
         rdma(full.at[p], full.at[p], ag_s.at[p], ag_r.at[p], tensor=1 - x).wait_recv()
-    for q in range(plane):
-        out[:, q * hid : (q + 1) * hid] = full[q]
+    acc[...] = jnp.dot(full[me], down_w[me], preferred_element_type=F32)
+    if n > 2:
+        w_step(n - 1)
+    for k in range(1, n):
+        b = nearest(me, k, n)
+        w_side_wait(b)
+        acc[...] += jnp.dot(full[b], down_w[b], preferred_element_type=F32)
+    out[...] = acc[...].astype(BF16)
 
     for b in range(n):
         @pl.when((b <= me) & (me + 1 < n))
@@ -286,6 +357,17 @@
         @pl.when(b != me)
         def _():
             comb_copy(b).wait_send()
+            for w in range(cuts):
+                w_side(b, w).wait_send()
+
+        for w in range(cuts):
+            @pl.when((b <= me) & (me + 1 < n))
+            def _():
+                w_right(b, w, down_w.at[b, span(w, y)]).wait_send()
+
+            @pl.when((b >= me) & (me >= 1))
+            def _():
+                w_left(b, w, down_w.at[b, span(w, y)]).wait_send()
 
     for step in range(1, n):
         gate_copy(step).wait_send()
@@ -293,7 +375,7 @@
         ag_copy(step).wait_send()
 
 
-def hidden_of(tokens, dense_gates, base_weights, in_factor, out_factors, ranks):
+def layer(tokens, dense_gates, base_weights, in_factor, out_factors, ranks):
     rows, feat = tokens.shape
     n = lax.axis_size("expert")
     plane = lax.axis_size("tensor") * lax.axis_size("inner")
@@ -308,11 +390,12 @@
     place = lax.broadcasted_iota(jnp.int32, (local, packed), 1)
     mask = ((place < ends) & (place >= ends - ranks[:, None])).astype(F32)
     two, four = rows // 2, rows // 4
+    cuts = 2
     vmem = pltpu.VMEM
     dma = pltpu.SemaphoreType.DMA
     return pl.pallas_call(
         functools.partial(fused, n, plane),
-        out_shape=jax.ShapeDtypeStruct((rows, plane * hid), BF16),
+        out_shape=jax.ShapeDtypeStruct((rows, feat), BF16),
         in_specs=[
             pl.BlockSpec(memory_space=pl.ANY),
             pl.BlockSpec(memory_space=vmem),
@@ -340,13 +423,16 @@
             vmem((n, rows, hid), BF16),
             vmem((n, rows, hid), BF16),
             vmem((plane, rows, hid), BF16),
-            dma((5,)),
+            vmem((n, unit, feat), BF16),
+            vmem((rows, feat), F32),
+            dma((6,)),
             dma((n,)), dma((n,)), dma((n,)), dma((n,)), dma((n,)),
             dma((n,)), dma((n,)), dma((n,)), dma((n,)), dma((n,)), dma((n,)), dma((n,)), dma((n,)),
             dma((n, n)), dma((n, plane)), dma((n,)), dma((n,)), dma((plane,)), dma((plane,)),
+            dma((n, cuts)), dma((n, cuts)), dma((n, cuts)), dma((n, cuts)), dma((n, cuts)),
         ],
         compiler_params=pltpu.CompilerParams(
-            collective_id=0, has_side_effects=True, vmem_limit_bytes=48 * 1024 * 1024
+            collective_id=0, has_side_effects=True, vmem_limit_bytes=60 * 1024 * 1024
         ),
         cost_estimate=pl.CostEstimate(
             flops=60_000_000_000, bytes_accessed=20_000_000, transcendentals=0
@@ -364,17 +450,14 @@
     hidden_slice = out_factors.shape[2]
     rows = tok_rows * owners
 
-    down = lax.all_gather(base_weights[2], "expert", axis=0, tiled=True)
-
     columns = lax.broadcasted_iota(jnp.int32, (1, 1, experts), 2)
     chosen = expert_ids[:, :, None] == columns
     dense_gates = jnp.sum(jnp.where(chosen, gate_weights[:, :, None], 0.0), axis=1)
     tensor, inner = lax.axis_size("tensor"), lax.axis_size("inner")
-    if tensor == 2 and inner == 2 and owners == tensor * inner and tok_rows % 64 == 0:
-        full_hidden = hidden_of(
-            tokens, dense_gates, base_weights, in_factor, out_factors, ranks
-        )
-        return jnp.dot(full_hidden, down, preferred_element_type=jnp.float32).astype(jnp.bfloat16)
+    square = tensor == 2 and inner == 2 and owners == tensor * inner
+    if square and lax.axis_size("groups") == 2 and tok_rows % 64 == 0 and hidden_rows % 64 == 0:
+        return layer(tokens, dense_gates, base_weights, in_factor, out_factors, ranks)
+    down = lax.all_gather(base_weights[2], "expert", axis=0, tiled=True)
     all_tokens = lax.all_gather(tokens, "expert", axis=0, tiled=True)
     all_gates = lax.all_gather(dense_gates, "expert", axis=0, tiled=True)
     own_gates = lax.dynamic_slice_in_dim(

time: 154 us -> 111 us (0.72)
  the two profiles are of different devices: /device:TPU:0 before, /device:TPU:2 now
where the time goes in v3:
time: 111 us; the launch traced here: 110 us
  Pallas kernels  105 us (95%)
  other arithmetic  3.44 us (3%)
  local copies, waits for them, and re-layouts  1.82 us (2%)
    pallas_call x1, Pallas kernels, layer(): pl.pallas_call(functools.partial(fused, n, plane), out_shape=jax.ShapeDty...  105 us

profile of v3, /device:TPU:2, one launch (start us, length us, event | category | flops | bytes accessed | tf_op | source)
XLA Modules:
  0.0 110.3 jit_solution(7878283908434280720)
XLA Ops:
  0.0 0.8 select_reduce_fusion.1
  0.8 0.7 sub.4
  1.4 1.3 %select_reduce_fusion = f32[128,32]{0,1:T(8,128)} fusion(f32[128,8]{0,1:T(8,128)} %param.9, s32[128,8]{0,1:T(8,128)} %param.8), kind=kLoop, calls=%fused_computation | loop fusion | flops 94208 | bytes 24576 | tf_op jit(solution)/shard_map/reduce_sum | solution.py:455
  2.8 0.7 fusion.1.mask
  3.4 105.0 %shard_map.73 = bf16[128,1792]{1,0:T(8,128)(2,1)} custom-call(bf16[128,1792]{1,0:T(8,128)(2,1)} %tokens.1, f32[32,128]{1,0:T(8,128)} %bitcast.1, f32[8,960]{1,0:T(8,128)} %fusion.1.mask, bf16[3,256,1792]{2,1,0:T(8,128)(2,1)} %base_weights.1, bf16[960,1792]{1,0:T(8,128)(2,1)} %in_factor.1, bf16[2,960,256]{2,1,0:T(8,128)(2,1)} %out_factors.1), custom_call_target="tpu_custom_call" | custom-call | flops 60000002048 | bytes 20000000 | tf_op jit(solution)/shard_map/pallas_call | solution.py:396
  108.5 1.8 %copy.11 = bf16[128,1792]{1,0:T(8,128)(2,1)} copy(bf16[128,1792]{1,0:T(8,128)(2,1)} %shard_map.73) | data formatting | bytes 917504

commit v4 on v3

--- a/solution.py
+++ b/solution.py
@@ -151,14 +151,21 @@
             spot = down_w.at[b, span(w, 1 - y)]
             rdma(spot, spot, wy_s.at[b, w], wy_got.at[b, w], groups=1 - y).wait_recv()
 
-    def w_begin():
-        for w in range(cuts):
-            @pl.when(me + 1 < n)
-            def _():
+    def reach(k):
+        d = nearest(me, jnp.minimum(k, n - 1), n) - me
+        return jnp.where(k >= n, n, jnp.maximum(d, -d))
+
+    def w_begin(k):
+        now, before = reach(k), reach(jnp.maximum(k - 1, 0))
+
+        @pl.when((me + 1 < n) & (now >= me + 1) & (before < me + 1))
+        def _():
+            for w in range(cuts):
                 w_right(me, w, down_w.at[me, span(w, y)]).start()
 
-            @pl.when(me >= 1)
-            def _():
+        @pl.when((me >= 1) & (now >= n - me) & (before < n - me))
+        def _():
+            for w in range(cuts):
                 w_left(me, w, down_w.at[me, span(w, y)]).start()
 
     def w_step(dist):
@@ -204,6 +211,7 @@
                 def _():
                     to_left(b, all_tok.at[b]).start()
 
+            w_begin(k)
             t = all_tok[b]
             nt = (((1,), (1,)), ((), ()))
             value = lax.dot_general(t, in_w[...], nt, preferred_element_type=F32).astype(BF16)
@@ -214,6 +222,14 @@
                 value = lax.dot_general(t, base_w[g], nt, preferred_element_type=F32)
                 part[b, :, wide + g * unit : wide + (g + 1) * unit] = value.astype(BF16)
             a_copy(b).start()
+
+        @pl.when(k == n)
+        def _():
+            w_begin(n)
+
+        @pl.when(k == n + 1)
+        def _():
+            w_step(1)
 
         @pl.when((k >= 1) & (k <= n))
         def _():
@@ -263,7 +279,6 @@
         return carry
 
     lax.fori_loop(0, n + 2, phase, 0)
-    w_begin()
 
     for step in range(1, n):
         p = lax.rem(me + step, n)
@@ -294,7 +309,7 @@
         for j in range(local):
             v = gate_base + delta[b, j, :, 0:hid].astype(F32)
             u = up_base + delta[b, j, :, hid : 2 * hid].astype(F32)
-            total = total + weight[:, j : j + 1] * (v / (1.0 + jnp.exp(-v)) * u)
+            total = total + weight[:, j : j + 1] * (v * (0.5 + 0.5 * jnp.tanh(0.5 * v)) * u)
         comb[b] = total.astype(BF16)
 
         @pl.when(b != me)
@@ -304,7 +319,8 @@
         return carry
 
     lax.fori_loop(0, n - 1, finish, 0)
-    w_step(1)
+    for dist in range(2, n - 1):
+        w_step(dist)
     finish(n - 1, 0)
 
     total = comb[me].astype(F32)
@@ -322,8 +338,6 @@
 
     for step in range(1, plane):
         ag_copy(step).start()
-    for dist in range(2, n - 1):
-        w_step(dist)
     for step in range(1, plane):
         p = lax.rem(ti + step, plane)
         rdma(full.at[p], full.at[p], ag_s.at[p], ag_r.at[p], tensor=1 - x).wait_recv()

time: 111 us -> 109 us (0.982)
  the two profiles are of different devices: /device:TPU:2 before, /device:TPU:0 now
where the time goes in v4:
time: 109 us
  Pallas kernels  104 us (95%)
  other arithmetic  3.44 us (3%)
  local copies, waits for them, and re-layouts  1.82 us (2%)
    pallas_call x1, Pallas kernels, layer(): pl.pallas_call(functools.partial(fused, n, plane), out_shape=jax.ShapeDty...  104 us

profile of v4, /device:TPU:0, one launch (start us, length us, event | category | flops | bytes accessed | tf_op | source)
XLA Modules:
  0.0 109.1 jit_solution(10336642841937231264)
XLA Ops:
  0.0 0.8 select_reduce_fusion.1
  0.8 0.7 sub.4
  1.4 1.3 %select_reduce_fusion = f32[128,32]{0,1:T(8,128)} fusion(f32[128,8]{0,1:T(8,128)} %param.9, s32[128,8]{0,1:T(8,128)} %param.8), kind=kLoop, calls=%fused_computation | loop fusion | flops 94208 | bytes 24576 | tf_op jit(solution)/shard_map/reduce_sum | solution.py:469
  2.8 0.7 fusion.1.mask
  3.4 103.9 %shard_map.73 = bf16[128,1792]{1,0:T(8,128)(2,1)} custom-call(bf16[128,1792]{1,0:T(8,128)(2,1)} %tokens.1, f32[32,128]{1,0:T(8,128)} %bitcast.1, f32[8,960]{1,0:T(8,128)} %fusion.1.mask, bf16[3,256,1792]{2,1,0:T(8,128)(2,1)} %base_weights.1, bf16[960,1792]{1,0:T(8,128)(2,1)} %in_factor.1, bf16[2,960,256]{2,1,0:T(8,128)(2,1)} %out_factors.1), custom_call_target="tpu_custom_call" | custom-call | flops 60000002048 | bytes 20000000 | tf_op jit(solution)/shard_map/pallas_call | solution.py:410
  107.3 1.8 %copy.11 = bf16[128,1792]{1,0:T(8,128)(2,1)} copy(bf16[128,1792]{1,0:T(8,128)(2,1)} %shard_map.73) | data formatting | bytes 917504

commit v5 on v4

--- a/solution.py
+++ b/solution.py
@@ -318,9 +318,15 @@
 
         return carry
 
+    middle = (me >= 1) & (me + 1 < n)
+
+    def w_middle():
+        for dist in range(2, n - 1):
+            w_step(dist)
+
+    pl.when(middle)(w_middle)
     lax.fori_loop(0, n - 1, finish, 0)
-    for dist in range(2, n - 1):
-        w_step(dist)
+    pl.when(jnp.logical_not(middle))(w_middle)
     finish(n - 1, 0)
 
     total = comb[me].astype(F32)
@@ -404,7 +410,7 @@
     place = lax.broadcasted_iota(jnp.int32, (local, packed), 1)
     mask = ((place < ends) & (place >= ends - ranks[:, None])).astype(F32)
     two, four = rows // 2, rows // 4
-    cuts = 2
+    cuts = 4
     vmem = pltpu.VMEM
     dma = pltpu.SemaphoreType.DMA
     return pl.pallas_call(
@@ -469,7 +475,7 @@
     dense_gates = jnp.sum(jnp.where(chosen, gate_weights[:, :, None], 0.0), axis=1)
     tensor, inner = lax.axis_size("tensor"), lax.axis_size("inner")
     square = tensor == 2 and inner == 2 and owners == tensor * inner
-    if square and lax.axis_size("groups") == 2 and tok_rows % 64 == 0 and hidden_rows % 64 == 0:
+    if square and lax.axis_size("groups") == 2 and tok_rows % 64 == 0 and hidden_rows % 128 == 0:
         return layer(tokens, dense_gates, base_weights, in_factor, out_factors, ranks)
     down = lax.all_gather(base_weights[2], "expert", axis=0, tiled=True)
     all_tokens = lax.all_gather(tokens, "expert", axis=0, tiled=True)

time: 109 us -> 110 us (level)
  no operation moved by 1% of the time
where the time goes in v5:
time: 110 us; the launch traced here: 109 us
  Pallas kernels  104 us (95%)
  other arithmetic  3.44 us (3%)
  local copies, waits for them, and re-layouts  1.82 us (2%)
    pallas_call x1, Pallas kernels, layer(): pl.pallas_call(functools.partial(fused, n, plane), out_shape=jax.ShapeDty...  104 us

profile of v5, /device:TPU:0, one launch (start us, length us, event | category | flops | bytes accessed | tf_op | source)
XLA Modules:
  0.0 109.4 jit_solution(1110356814137840774)
XLA Ops:
  0.0 0.8 select_reduce_fusion.1
  0.8 0.7 sub.4
  1.4 1.3 %select_reduce_fusion = f32[128,32]{0,1:T(8,128)} fusion(f32[128,8]{0,1:T(8,128)} %param.9, s32[128,8]{0,1:T(8,128)} %param.8), kind=kLoop, calls=%fused_computation | loop fusion | flops 94208 | bytes 24576 | tf_op jit(solution)/shard_map/reduce_sum | solution.py:475
  2.8 0.7 fusion.1.mask
  3.4 104.2 %shard_map.73 = bf16[128,1792]{1,0:T(8,128)(2,1)} custom-call(bf16[128,1792]{1,0:T(8,128)(2,1)} %tokens.1, f32[32,128]{1,0:T(8,128)} %bitcast.1, f32[8,960]{1,0:T(8,128)} %fusion.1.mask, bf16[3,256,1792]{2,1,0:T(8,128)(2,1)} %base_weights.1, bf16[960,1792]{1,0:T(8,128)(2,1)} %in_factor.1, bf16[2,960,256]{2,1,0:T(8,128)(2,1)} %out_factors.1), custom_call_target="tpu_custom_call" | custom-call | flops 60000002048 | bytes 20000000 | tf_op jit(solution)/shard_map/pallas_call | solution.py:416
  107.6 1.8 %copy.11 = bf16[128,1792]{1,0:T(8,128)(2,1)} copy(bf16[128,1792]{1,0:T(8,128)(2,1)} %shard_map.73) | data formatting | bytes 917504
